TPU v7x, 128 devices: a whole 4x4x4 slice. The times are simulated.
128 devices in a mesh: seq: 16 (over y, x), mp: 8 (over z, core).
Axes of the slice: x: 4, y: 4, z: 4, core: 2. Of those that a mesh axis runs over, the one named last changes fastest.
Arguments:
- residual_activations: bfloat16 [16384, 4096], P('seq', 'mp'), may hold values from -6 to 6
- prelayer_gain_vector: bfloat16 [4096], replicated, may hold values from 0.099609375 to 1.8984375
- gating_projection: bfloat16 [4096], replicated, may hold values from -0.25 to 0.25
- asker_projection: bfloat16 [4096, 8192], P(None, 'mp'), may hold values from -0.09375 to 0.09375
- lookup_projection: bfloat16 [4096, 1024], P(None, 'mp'), may hold values from -0.09375 to 0.09375
- content_projection: bfloat16 [4096, 1024], P(None, 'mp'), may hold values from -0.09375 to 0.09375
- final_projection: bfloat16 [8192, 4096], P(None, 'mp'), may hold values from -0.0625 to 0.0625
- logit_sharpness: float32 [64], P('mp'), may hold values from 1 to 64
- selection_table: int32 [16, 256], P('seq'), may hold values from 0 to 1023, as said below
- dispatched_tally_table: int32 [16, 16], replicated, may hold values from 0 to 16, as said below
Outputs:
- blended: bfloat16 [16384, 4096], P('seq', 'mp')
Inputs may be any that keep to these rules, and one draw needn't show every extreme that they name: `dispatched_tally_table`: entry [s, d] counts the routed tokens of source shard s whose compacted place falls to owner d: the compacted sequence lists all routed tokens in sequence order and is dealt in blocks of 8 places, block b to owner b mod 16. Every entry is a multiple of 8, and every column sums to 128. `selection_table`: row s lists in increasing order the distinct local indices of the routed tokens of source shard s, as many as row s of dispatched_tally_table sums to, and zeros after them.
All inputs are finite; a program needn't handle non-finite values.
Results may differ from a plain program's by a relative error of at most 0.0059.
Values may be sent and summed in bfloat16 or wider, within the bound.
No kernel may reach another device: no remote copies, remote signals or barrier semaphores. Data moves between devices by JAX's collectives and lax.ppermute only.
A program may use at most 64 MiB of HBM per device.

v0:
```python
import math
import jax
import jax.numpy as jnp
from jax import lax
from jax.sharding import PartitionSpec as P

HEADS = 64
SHARED_KV_COUNT = 8
PER_HEAD_DIM = 128
SEL = 128


def compact(incoming, prefix, spans, shard, nseq, owned):
    span_ids = jnp.arange(nseq, dtype=jnp.int32) * nseq + shard
    source_of = jnp.sum(
        (prefix[None, :] + spans[None, :] <= span_ids[:, None]).astype(jnp.int32), axis=1
    )
    matches = source_of[:, None] == jnp.arange(nseq, dtype=jnp.int32)[None, :]
    start_of = jnp.sum(jnp.where(matches, prefix[None, :], 0), axis=1)
    half_of = (span_ids - start_of) // nseq
    blocks = incoming.reshape(2 * nseq, incoming.shape[2], incoming.shape[3])
    return blocks[half_of * nseq + source_of].reshape(owned, incoming.shape[3])


def build_return(delta, prefix, spans, shard, nseq, block_rows):
    first = (shard - prefix) % nseq
    counter = jnp.arange(2, dtype=jnp.int32)[:, None] * nseq + first[None, :]
    usable = counter < spans[None, :]
    target = jnp.minimum((prefix[None, :] + counter) // nseq, nseq - 1)
    blocks = delta.reshape(nseq, block_rows, delta.shape[1])[target]
    return jnp.where(usable[:, :, None, None], blocks, jnp.zeros_like(blocks))


def on_device(
    residual_activations,
    prelayer_gain_vector,
    gating_projection,
    asker_projection,
    lookup_projection,
    content_projection,
    final_projection,
    logit_sharpness,
    selection_table,
    dispatched_tally_table,
):
    nseq = lax.axis_size("seq")
    shard = lax.axis_index("seq")
    owned = SEL
    block_rows = owned // nseq
    slots = selection_table.shape[1]
    sent = jnp.sum(dispatched_tally_table, axis=1)
    spans = sent // block_rows
    prefix = jnp.cumsum(spans) - spans
    mine = jnp.arange(nseq, dtype=jnp.int32) == shard
    my_prefix = jnp.sum(jnp.where(mine, prefix, 0))
    my_sent = jnp.sum(jnp.where(mine, sent, 0))
    rotation = my_prefix % nseq
    index_list = selection_table[0]
    live = jnp.arange(slots) < my_sent
    gathered_rows = residual_activations[index_list]
    gathered_rows = jnp.where(live[:, None], gathered_rows, jnp.zeros_like(gathered_rows))
    whole_rows = lax.all_gather(gathered_rows, "mp", axis=1, tiled=True)
    outgoing = jnp.roll(
        whole_rows.reshape(2, nseq, block_rows, whole_rows.shape[1]), rotation, axis=1
    )
    incoming = lax.all_to_all(outgoing, "seq", split_axis=1, concat_axis=1, tiled=True)
    full = compact(incoming, prefix, spans, shard, nseq, owned)
    gate = jax.nn.sigmoid(jnp.dot(full, gating_projection, preferred_element_type=jnp.float32))
    widened = full.astype(jnp.float32)
    inverse = lax.rsqrt(jnp.mean(widened * widened, axis=1, keepdims=True) + 1e-05)
    normed = (widened * inverse * prelayer_gain_vector.astype(jnp.float32)).astype(jnp.bfloat16)
    query = jnp.dot(normed, asker_projection, preferred_element_type=jnp.float32).astype(
        jnp.bfloat16
    )
    keys = jnp.dot(normed, lookup_projection, preferred_element_type=jnp.float32).astype(
        jnp.bfloat16
    )
    values = jnp.dot(normed, content_projection, preferred_element_type=jnp.float32).astype(
        jnp.bfloat16
    )
    paired = jnp.stack([keys, values])
    memory_pair_portion = lookup_projection.shape[1] // PER_HEAD_DIM
    asker_cluster = HEADS // SHARED_KV_COUNT
    query_heads = query.reshape(owned, memory_pair_portion, asker_cluster, PER_HEAD_DIM)
    gating_multipliers = logit_sharpness.reshape(memory_pair_portion, asker_cluster) / math.sqrt(
        PER_HEAD_DIM
    )
    own_slots = jnp.arange(owned, dtype=jnp.int32)
    query_places = (
        own_slots // block_rows * nseq * block_rows + shard * block_rows + own_slots % block_rows
    )
    start_best = jnp.full((memory_pair_portion, asker_cluster, owned), -1e30, jnp.float32)
    piece = lax.all_gather(paired, "seq", axis=1, tiled=True)
    best = start_best
    count = piece.shape[1]
    key_piece = piece[0].reshape(count, memory_pair_portion, PER_HEAD_DIM)
    value_piece = piece[1].reshape(count, memory_pair_portion, PER_HEAD_DIM)
    index_all = jnp.arange(count, dtype=jnp.int32)
    owner = index_all // owned
    position = index_all % owned
    key_places = (
        position // block_rows * nseq * block_rows + owner * block_rows + position % block_rows
    )
    allowed = key_places[None, :] <= query_places[:, None]
    score = jnp.einsum("qngd,knd->ngqk", query_heads, key_piece, preferred_element_type=jnp.float32)
    score = jnp.where(allowed[None, None], score * gating_multipliers[:, :, None, None], -1e30)
    new_best = jnp.maximum(best, jnp.max(score, axis=3))
    weights = jnp.where(allowed[None, None], jnp.exp(score - new_best[..., None]), 0.0)
    totals = jnp.sum(weights, axis=3)
    mixed = jnp.einsum(
        "ngqk,knd->ngqd",
        weights.astype(jnp.bfloat16),
        value_piece,
        preferred_element_type=jnp.float32,
    )
    sums = mixed
    best, totals, sums = (new_best, totals, sums)
    attended = (sums / totals[..., None]).astype(jnp.bfloat16)
    attended = attended.transpose(2, 0, 1, 3).reshape(
        owned, memory_pair_portion * asker_cluster * PER_HEAD_DIM
    )
    projected = jnp.dot(
        lax.all_gather(attended, "mp", axis=1, tiled=True),
        final_projection,
        preferred_element_type=jnp.float32,
    )
    delta = (gate[:, None] * projected).astype(jnp.bfloat16)
    outgoing_back = build_return(delta, prefix, spans, shard, nseq, block_rows)
    coming_back = lax.all_to_all(outgoing_back, "seq", split_axis=1, concat_axis=1, tiled=True)
    restored = jnp.roll(coming_back, -rotation, axis=1).reshape(slots, delta.shape[1])
    restored = jnp.where(live[:, None], restored, jnp.zeros_like(restored))
    updated = (
        residual_activations.astype(jnp.float32).at[index_list].add(restored.astype(jnp.float32))
    )
    return updated.astype(jnp.bfloat16)


def solution(mesh):
    placed = (
        P("seq", "mp"),
        P(),
        P(),
        P(None, "mp"),
        P(None, "mp"),
        P(None, "mp"),
        P(None, "mp"),
        P("mp"),
        P("seq", None),
        P(),
    )
    return jax.shard_map(
        on_device, mesh=mesh, in_specs=placed, out_specs=P("seq", "mp"), check_vma=False
    )
```

profile of v0, /device:TPU:1, one launch (start us, length us, event | category | flops | bytes accessed | tf_op | source)
XLA Modules:
  0.0 201.7 jit_solution(617594323271170253)
XLA Ops:
  6.5 0.9 reduce_sum.69
  9.7 2.6 %gather_fusion = bf16[256,512]{1,0:T(8,128)(2,1)S(1)} fusion(bf16[1024,512]{1,0:T(8,128)(2,1)} %param.10, s32[1024]{0:T(1024)S(1)} %pad_clamp_fusion.2), kind=kCustom, calls=%fused_computation | custom fusion | bytes 525312 | tf_op jit(solution)/shard_map/gather | solution.py:60
  12.3 0.8 broadcast_select_fusion
  15.6 26.6 %all-gather.4.cloned.1.call-done = bf16[256,4096]{1,0:T(8,128)(2,1)} async-done(((bf16[256,512]{1,0:T(8,128)(2,1)}), bf16[256,4096]{1,0:T(8,128)(2,1)}) %all-gather.4.cloned.1.call-update) | async-done | bytes 2097168 | tf_op jit(solution)/shard_map/all_gather | solution.py:62
  42.3 2.4 %fusion.7 = bf16[2,16,8,4096]{3,2,1,0:T(8,128)(2,1)S(1)} fusion(s32[]{:T(128)S(6)} %select_n.208, bf16[2,16,8,4096]{3,2,1,0:T(8,128)(2,1)} %bitcast.124), kind=kLoop, calls=%fused_computation.15 | loop fusion | flops 1048576 | bytes 4194308 | tf_op jit(solution)/shard_map/jit(_roll_dynamic)/concatenate | solution.py:63
  44.6 1.5 copy.48
  46.1 6.6 %all-to-all-start = ((bf16[2,16,8,4096]{3,2,0,1:T(8,128)(2,1)}), bf16[2,16,8,4096]{3,2,0,1:T(8,128)(2,1)S(1)}, u32[]{:S(2)}, u32[]{:S(2)}) async-start(bf16[2,16,8,4096]{3,2,0,1:T(8,128)(2,1)} %copy.48), calls=%async_computation | async-start | bytes 4194304 | tf_op jit(solution)/shard_map/all_to_all | solution.py:66
  53.2 32.2 %all-to-all-done = bf16[2,16,8,4096]{3,2,0,1:T(8,128)(2,1)S(1)} async-done(((bf16[2,16,8,4096]{3,2,0,1:T(8,128)(2,1)}), bf16[2,16,8,4096]{3,2,0,1:T(8,128)(2,1)S(1)}, u32[]{:S(2)}, u32[]{:S(2)}) %all-to-all-start) | async-done | bytes 2097184 | tf_op jit(solution)/shard_map/all_to_all | solution.py:66
  85.4 1.5 copy.38
  86.9 2.2 %gather_fusion.1 = bf16[16,8,4096]{2,1,0:T(8,128)(2,1)S(1)} fusion(bf16[32,8,4096]{2,1,0:T(8,128)(2,1)} %bitcast.123, s32[1024]{0:T(1024)S(1)} %pad_clamp_fusion.1), kind=kCustom, calls=%fused_computation.1 | custom fusion | bytes 2097216 | tf_op jit(solution)/shard_map/gather | solution.py:22
  90.0 1.7 fusion.12
  92.9 4.7 %fusion.8 = bf16[16,8,8,128]{3,2,1,0:T(8,128)(2,1)S(1)} fusion(bf16[4096,1024]{1,0:T(8,128)(2,1)} %param.13, bf16[16,8,4096]{2,1,0:T(8,128)(2,1)S(1)} %gather_fusion.1, f32[4096]{0:T(1024)S(1)} %convert_element_type.49, f32[128]{0:T(128)S(1)} %rsqrt.12), kind=kOutput, calls=%fused_computation.20 | convolution fusion | flops 1075970048 | bytes 9716224 | tf_op jit(solution)/shard_map/dot_general | solution.py:72
  97.6 34.0 %all-gather.6.cloned.1.call-done = bf16[2,2048,128]{2,1,0:T(8,128)(2,1)} async-done(((bf16[2,128,128]{2,1,0:T(8,128)(2,1)}), bf16[2,2048,128]{2,1,0:T(8,128)(2,1)}) %all-gather.6.cloned.1.call-update) | async-done | bytes 1048592 | tf_op jit(solution)/shard_map/all_gather | solution.py:93
  131.6 2.3 %fusion = (f32[8,128]{1,0:T(8,128)S(1)}, f32[2048,128,8]{1,0,2:T(8,128)S(1)}) fusion(f32[8]{0:T(128)S(1)} %broadcast_multiply_fusion, pred[128,2048]{0,1:T(8,128)(4,1)S(1)} %broadcast_compare_fusion, bf16[16,8,8,128]{3,2,1,0:T(8,128)(2,1)S(1)} %fusion.8, bf16[2,2048,128]{2,1,0:T(8,128)(2,1)} %all-gather.6.cloned.1.call-done), kind=kOutput, calls=%fused_computation.7 | convolution fusion | flops 543161344 | bytes 9441312 | tf_op jit(solution)/shard_map/qngd,knd->ngqk/dot_general | solution.py:105
  133.9 2.1 %fusion.1 = f32[8,128]{1,0:T(8,128)S(1)} fusion(f32[2048,128,8]{1,0,2:T(8,128)S(1)} %get-tuple-element.10, f32[8,128]{1,0:T(8,128)S(1)} %broadcast_maximum_fusion, f32[8]{0:T(128)S(1)} %broadcast_multiply_fusion, pred[128,2048]{0,1:T(8,128)(4,1)S(1)} %broadcast_compare_fusion), kind=kLoop, calls=%fused_computation.8 | loop fusion | flops 10484736 | bytes 8658976 | tf_op jit(solution)/shard_map/reduce_sum | solution.py:109
  136.0 2.8 %fusion.21 = bf16[8,128,128]{1,2,0:T(8,128)(2,1)} fusion(f32[2048,128,8]{1,0,2:T(8,128)S(1)} %get-tuple-element.10, f32[8,128]{1,0:T(8,128)S(1)} %broadcast_maximum_fusion, f32[8]{0:T(128)S(1)} %broadcast_multiply_fusion, pred[128,2048]{0,1:T(8,128)(4,1)S(1)} %broadcast_compare_fusion, bf16[2,2048,128]{2,1,0:T(8,128)(2,1)S(1)} %copy-done.2, ...), kind=kOutput, calls=%fused_computation.34 | convolution fusion | flops 547618816 | bytes 9445888 | tf_op jit(solution)/shard_map/ngqk,knd->ngqd/dot_general | solution.py:110
  139.5 26.0 %all-gather.8.cloned.1.call-done = bf16[128,8192]{0,1:T(8,128)(2,1)} async-done(((bf16[128,1024]{0,1:T(8,128)(2,1)}), bf16[128,8192]{0,1:T(8,128)(2,1)}) %all-gather.8.cloned.1.call-update) | async-done | bytes 2097168 | tf_op jit(solution)/shard_map/all_gather | solution.py:123
  165.5 5.3 %fusion.10 = bf16[16,8,512]{2,1,0:T(8,128)(2,1)S(1)} fusion(bf16[128,8192]{0,1:T(8,128)(2,1)} %all-gather.8.cloned.1.call-done, bf16[8192,512]{1,0:T(8,128)(2,1)} %param.16, f32[128]{0:T(128)S(1)} %fusion.16), kind=kOutput, calls=%fused_computation.22 | convolution fusion | flops 1073872896 | bytes 10617344 | tf_op jit(solution)/shard_map/dot_general | solution.py:122
  171.5 0.7 copy.42
  172.3 6.5 %all-to-all-start.1 = ((bf16[2,16,8,512]{3,2,0,1:T(8,128)(2,1)}), bf16[2,16,8,512]{3,2,0,1:T(8,128)(2,1)S(1)}, u32[]{:S(2)}, u32[]{:S(2)}) async-start(bf16[2,16,8,512]{3,2,0,1:T(8,128)(2,1)} %copy.42), calls=%async_computation.1 | async-start | bytes 524288 | tf_op jit(solution)/shard_map/all_to_all | solution.py:129
  178.8 1.6 convert_element_type.45
  180.5 6.6 %all-to-all-done.1 = bf16[2,16,8,512]{3,2,0,1:T(8,128)(2,1)S(1)} async-done(((bf16[2,16,8,512]{3,2,0,1:T(8,128)(2,1)}), bf16[2,16,8,512]{3,2,0,1:T(8,128)(2,1)S(1)}, u32[]{:S(2)}, u32[]{:S(2)}) %all-to-all-start.1) | async-done | bytes 262176 | tf_op jit(solution)/shard_map/all_to_all | solution.py:129
  187.3 5.2 %scatter_custom_fusion = f32[1024,512]{1,0:T(8,128)} fusion(f32[1024,512]{1,0:T(8,128)} %convert_element_type.45, s32[256]{0:T(256)S(1)} %bitcast.128, bf16[256,512]{1,0:T(8,128)(2,1)S(1)} %bitcast_select_fusion.1), kind=kCustom, calls=%fused_computation.40 | custom fusion | flops 262144 | bytes 2359296 | tf_op jit(solution)/shard_map/scatter-add | solution.py:133
  192.5 2.7 %convert_element_type.59 = bf16[1024,512]{1,0:T(8,128)(2,1)} convert(f32[1024,512]{1,0:T(8,128)} %scatter_custom_fusion) | non-fusion elementwise | flops 524288 | bytes 3145728 | tf_op jit(solution)/shard_map/convert_element_type | solution.py:135
  (54 shorter events, 6.9 us)
Async XLA Ops:
  6.5 82.9 %copy-start = (bf16[4096,128]{1,0:T(8,128)(2,1)S(1)}, bf16[4096,128]{1,0:T(8,128)(2,1)}, u32[]{:S(2)}) copy-start(bf16[4096,128]{1,0:T(8,128)(2,1)} %param.14) | copy-start | bytes 3145732
  6.5 35.7 %all-gather.4.cloned.1.call-start = ((), (), s32[]{:S(2)}) async-start(), calls=%async_computation.2 | async-start | bytes 2359296 | tf_op jit(solution)/shard_map/all_gather | solution.py:62
  46.1 6.7 %copy-start.3 = (bf16[4096]{0:T(1024)(128)(2,1)S(1)}, bf16[4096]{0:T(1024)(128)(2,1)}, u32[]{:S(2)}) copy-start(bf16[4096]{0:T(1024)(128)(2,1)} %param.11) | copy-start | bytes 24580
  46.1 39.3 %all-to-all-start = ((bf16[2,16,8,4096]{3,2,0,1:T(8,128)(2,1)}), bf16[2,16,8,4096]{3,2,0,1:T(8,128)(2,1)S(1)}, u32[]{:S(2)}, u32[]{:S(2)}) async-start(bf16[2,16,8,4096]{3,2,0,1:T(8,128)(2,1)} %copy.48), calls=%async_computation | async-start | bytes 4194304 | tf_op jit(solution)/shard_map/all_to_all | solution.py:66
  52.8 78.8 %all-gather.6.cloned.1.call-start = ((), (), s32[]{:S(2)}) async-start(), calls=%async_computation.3 | async-start | bytes 1114112 | tf_op jit(solution)/shard_map/all_gather | solution.py:93
  90.0 2.5 %copy-start.5 = (f32[8]{0:T(128)S(1)}, f32[8]{0:T(128)}, u32[]{:S(2)}) copy-start(f32[8]{0:T(128)} %param.17) | copy-start | bytes 100
  92.4 73.1 %all-gather.8.cloned.1.call-start = ((), (), s32[]{:S(2)}) async-start(), calls=%async_computation.4 | async-start | bytes 2359296 | tf_op jit(solution)/shard_map/all_gather | solution.py:123
  133.9 2.1 %copy-start.2 = (bf16[2,2048,128]{2,1,0:T(8,128)(2,1)S(1)}, bf16[2,2048,128]{2,1,0:T(8,128)(2,1)}, u32[]{:S(2)}) copy-start(bf16[2,2048,128]{2,1,0:T(8,128)(2,1)} %all-gather.6.cloned.1.call-done) | copy-start | bytes 3145732
  136.0 2.8 %copy-start.4 = (bf16[4096]{0:T(1024)(128)(2,1)S(1)}, bf16[4096]{0:T(1024)(128)(2,1)}, u32[]{:S(2)}) copy-start(bf16[4096]{0:T(1024)(128)(2,1)} %param.12) | copy-start | bytes 24580
  170.8 8.0 %copy-start.1 = (bf16[1024,512]{1,0:T(8,128)(2,1)S(1)}, bf16[1024,512]{1,0:T(8,128)(2,1)}, u32[]{:S(2)}) copy-start(bf16[1024,512]{1,0:T(8,128)(2,1)} %param.10) | copy-start | bytes 3145732
  172.3 14.8 %all-to-all-start.1 = ((bf16[2,16,8,512]{3,2,0,1:T(8,128)(2,1)}), bf16[2,16,8,512]{3,2,0,1:T(8,128)(2,1)S(1)}, u32[]{:S(2)}, u32[]{:S(2)}) async-start(bf16[2,16,8,512]{3,2,0,1:T(8,128)(2,1)} %copy.42), calls=%async_computation.1 | async-start | bytes 524288 | tf_op jit(solution)/shard_map/all_to_all | solution.py:129
Sparse Core Ops, SparseCore 0:
  13.2 29.0 all-gather.3
  92.5 38.9 all-gather.5
  139.0 26.4 all-gather.7
where the time goes:
time: 202 us
  waiting for transfers between devices  125 us (62%)
  other arithmetic  20.7 us (10%)
  matrix products  17.7 us (9%)
  between operations  15.3 us (8%)
  starting transfers between devices  13.2 us (7%)
  local copies, waits for them, and re-layouts  9.37 us (5%)
    all_gather x1, waiting for transfers between devices, on_device(): piece = lax.all_gather(paired, 'seq', axis=1, tiled=True)  34 us
    all_to_all x1, waiting for transfers between devices, on_device(): lax.all_to_all(outgoing, 'seq', split_axis=1, concat_axis=1, tiled=True)  32.2 us
    all_gather x1, waiting for transfers between devices, on_device(): whole_rows = lax.all_gather(gathered_rows, 'mp', axis=1, tiled=True)  26.6 us
    all_gather x1, waiting for transfers between devices, on_device(): lax.all_gather(attended, 'mp', axis=1, tiled=True)  26 us
    all_to_all x1, starting transfers between devices, on_device(): lax.all_to_all(outgoing, 'seq', split_axis=1, concat_axis=1, tiled=True)  6.64 us
    all_to_all x1, waiting for transfers between devices, on_device(): lax.all_to_all(outgoing_back, 'seq', split_axis=1, concat_axis=1, tiled=T...  6.56 us
    all_to_all x1, starting transfers between devices, on_device(): lax.all_to_all(outgoing_back, 'seq', split_axis=1, concat_axis=1, tiled=T...  6.52 us
    dot_general x1, matrix products, on_device(): jnp.dot(lax.all_gather(attended, 'mp', axis=1, tiled=True), final_project...  5.31 us
  transfers between devices with their start and end apart: 5, of which 5 were waited for; matrix products, arithmetic and copies ran while one was open for 4% of the time, Pallas kernels for 0%

commit v1 on v0

--- a/solution.py
+++ b/solution.py
@@ -8,6 +8,17 @@
 SHARED_KV_COUNT = 8
 PER_HEAD_DIM = 128
 SEL = 128
+
+
+def split_up(x, dim, count):
+    before, after = (x.shape[:dim], x.shape[dim + 1 :])
+    return jnp.moveaxis(x.reshape(*before, count, -1, *after), dim, 0)
+
+
+def in_order(parts, dim):
+    dims = list(parts.shape[1:])
+    dims[dim] *= parts.shape[0]
+    return jnp.moveaxis(parts, 0, dim).reshape(dims)
 
 
 def compact(incoming, prefix, spans, shard, nseq, owned):
@@ -126,7 +137,15 @@
     )
     delta = (gate[:, None] * projected).astype(jnp.bfloat16)
     outgoing_back = build_return(delta, prefix, spans, shard, nseq, block_rows)
-    coming_back = lax.all_to_all(outgoing_back, "seq", split_axis=1, concat_axis=1, tiled=True)
+    size, index = (lax.axis_size("seq"), lax.axis_index("seq"))
+    pieces = split_up(outgoing_back, 1, size)
+    out = pieces
+    for hop in range(1, size):
+        target_2, source = ((index + hop) % size, (index - hop) % size)
+        sent_2 = lax.dynamic_index_in_dim(pieces, target_2, 0)
+        other = lax.ppermute(sent_2, "seq", [(i, (i + hop) % size) for i in range(size)])
+        out = lax.dynamic_update_slice_in_dim(out, other, source, axis=0)
+    coming_back = in_order(out, 1)
     restored = jnp.roll(coming_back, -rotation, axis=1).reshape(slots, delta.shape[1])
     restored = jnp.where(live[:, None], restored, jnp.zeros_like(restored))
     updated = (

time: 202 us -> 216 us (1.069)
  the two profiles are of different devices: /device:TPU:1 before, /device:TPU:6 now
where the time goes in v1:
time: 216 us; the launch traced here: 215 us
  waiting for transfers between devices  119 us (55%)
  starting transfers between devices  36.3 us (17%)
  matrix products  17.7 us (8%)
  other arithmetic  16.9 us (8%)
  between operations  16 us (7%)
  local copies, waits for them, and re-layouts  8.88 us (4%)
    all_gather x1, waiting for transfers between devices, on_device(): piece = lax.all_gather(paired, 'seq', axis=1, tiled=True)  36.7 us
    all_to_all x1, waiting for transfers between devices, on_device(): lax.all_to_all(outgoing, 'seq', split_axis=1, concat_axis=1, tiled=True)  29.9 us
    ppermute x15, starting transfers between devices, on_device(): lax.ppermute(sent_2, 'seq', [(i, (i + hop) % size) for i in range(size)])  28.6 us
    all_gather x1, waiting for transfers between devices, on_device(): whole_rows = lax.all_gather(gathered_rows, 'mp', axis=1, tiled=True)  25.3 us
    all_gather x1, waiting for transfers between devices, on_device(): lax.all_gather(attended, 'mp', axis=1, tiled=True)  22.4 us
    all_to_all x1, starting transfers between devices, on_device(): lax.all_to_all(outgoing, 'seq', split_axis=1, concat_axis=1, tiled=True)  7.42 us
    dot_general x1, matrix products, on_device(): jnp.dot(lax.all_gather(attended, 'mp', axis=1, tiled=True), final_project...  5.31 us
    ppermute x15, waiting for transfers between devices, on_device(): lax.ppermute(sent_2, 'seq', [(i, (i + hop) % size) for i in range(size)])  5.17 us
  transfers between devices with their start and end apart: 19, of which 6 were waited for; matrix products, arithmetic and copies ran while one was open for 4% of the time, Pallas kernels for 0%

profile of v1, /device:TPU:6, one launch (start us, length us, event | category | flops | bytes accessed | tf_op | source)
XLA Modules:
  0.0 215.2 jit_solution(415130816733067745)
XLA Ops:
  9.7 2.6 %gather_fusion = bf16[256,512]{1,0:T(8,128)(2,1)S(1)} fusion(bf16[1024,512]{1,0:T(8,128)(2,1)} %param.10, s32[1024]{0:T(1024)S(1)} %pad_clamp_fusion.2), kind=kCustom, calls=%fused_computation | custom fusion | bytes 525312 | tf_op jit(solution)/shard_map/gather | solution.py:71
  15.7 25.3 %all-gather.4.cloned.1.call-done = bf16[256,4096]{1,0:T(8,128)(2,1)} async-done(((bf16[256,512]{1,0:T(8,128)(2,1)}), bf16[256,4096]{1,0:T(8,128)(2,1)}) %all-gather.4.cloned.1.call-update) | async-done | bytes 2097168 | tf_op jit(solution)/shard_map/all_gather | solution.py:73
  40.9 2.3 %fusion.7 = bf16[2,16,8,4096]{3,2,1,0:T(8,128)(2,1)S(1)} fusion(s32[]{:T(128)S(6)} %select_n.426, bf16[2,16,8,4096]{3,2,1,0:T(8,128)(2,1)} %bitcast.161), kind=kLoop, calls=%fused_computation.15 | loop fusion | flops 1048576 | bytes 4194308 | tf_op jit(solution)/shard_map/jit(_roll_dynamic)/concatenate | solution.py:74
  44.8 7.4 %all-to-all-start = ((bf16[2,16,8,4096]{3,2,0,1:T(8,128)(2,1)}), bf16[2,16,8,4096]{3,2,0,1:T(8,128)(2,1)S(1)}, u32[]{:S(2)}, u32[]{:S(2)}) async-start(bf16[2,16,8,4096]{3,2,0,1:T(8,128)(2,1)} %copy.43), calls=%async_computation | async-start | bytes 4194304 | tf_op jit(solution)/shard_map/all_to_all | solution.py:77
  52.7 29.9 %all-to-all-done = bf16[2,16,8,4096]{3,2,0,1:T(8,128)(2,1)S(1)} async-done(((bf16[2,16,8,4096]{3,2,0,1:T(8,128)(2,1)}), bf16[2,16,8,4096]{3,2,0,1:T(8,128)(2,1)S(1)}, u32[]{:S(2)}, u32[]{:S(2)}) %all-to-all-start) | async-done | bytes 2097184 | tf_op jit(solution)/shard_map/all_to_all | solution.py:77
  84.2 2.2 %gather_fusion.1 = bf16[16,8,4096]{2,1,0:T(8,128)(2,1)S(1)} fusion(bf16[32,8,4096]{2,1,0:T(8,128)(2,1)} %bitcast.158, s32[1024]{0:T(1024)S(1)} %pad_clamp_fusion.1), kind=kCustom, calls=%fused_computation.1 | custom fusion | bytes 2097216 | tf_op jit(solution)/shard_map/gather | solution.py:33
  87.3 1.7 fusion.12
  90.3 4.7 %fusion.8 = bf16[16,8,8,128]{3,2,1,0:T(8,128)(2,1)S(1)} fusion(bf16[4096,1024]{1,0:T(8,128)(2,1)} %param.13, bf16[16,8,4096]{2,1,0:T(8,128)(2,1)S(1)} %gather_fusion.1, f32[4096]{0:T(1024)S(1)} %convert_element_type.49, f32[128]{0:T(128)S(1)} %rsqrt.12), kind=kOutput, calls=%fused_computation.20 | convolution fusion | flops 1075970048 | bytes 9716224 | tf_op jit(solution)/shard_map/dot_general | solution.py:83
  95.0 36.7 %all-gather.6.cloned.1.call-done = bf16[2,2048,128]{2,1,0:T(8,128)(2,1)} async-done(((bf16[2,128,128]{2,1,0:T(8,128)(2,1)}), bf16[2,2048,128]{2,1,0:T(8,128)(2,1)}) %all-gather.6.cloned.1.call-update) | async-done | bytes 1048592 | tf_op jit(solution)/shard_map/all_gather | solution.py:104
  131.7 2.3 %fusion = (f32[8,128]{1,0:T(8,128)S(1)}, f32[2048,128,8]{1,0,2:T(8,128)S(1)}) fusion(f32[8]{0:T(128)S(1)} %broadcast_multiply_fusion, pred[128,2048]{0,1:T(8,128)(4,1)S(1)} %broadcast_compare_fusion, bf16[16,8,8,128]{3,2,1,0:T(8,128)(2,1)S(1)} %fusion.8, bf16[2,2048,128]{2,1,0:T(8,128)(2,1)} %all-gather.6.cloned.1.call-done), kind=kOutput, calls=%fused_computation.7 | convolution fusion | flops 543161344 | bytes 9441312 | tf_op jit(solution)/shard_map/qngd,knd->ngqk/dot_general | solution.py:116
  134.0 2.1 fusion.1
  136.2 2.8 %fusion.21 = bf16[8,128,128]{1,2,0:T(8,128)(2,1)} fusion(f32[2048,128,8]{1,0,2:T(8,128)S(1)} %get-tuple-element.25, f32[8,128]{1,0:T(8,128)S(1)} %broadcast_maximum_fusion, f32[8]{0:T(128)S(1)} %broadcast_multiply_fusion, pred[128,2048]{0,1:T(8,128)(4,1)S(1)} %broadcast_compare_fusion, bf16[2,2048,128]{2,1,0:T(8,128)(2,1)S(1)} %copy-done.3, ...), kind=kOutput, calls=%fused_computation.34 | convolution fusion | flops 547618816 | bytes 9445888 | tf_op jit(solution)/shard_map/ngqk,knd->ngqd/dot_general | solution.py:121
  139.5 1.6 convert_element_type.45
  141.9 22.4 %all-gather.8.cloned.1.call-done = bf16[128,8192]{0,1:T(8,128)(2,1)} async-done(((bf16[128,1024]{0,1:T(8,128)(2,1)}), bf16[128,8192]{0,1:T(8,128)(2,1)}) %all-gather.8.cloned.1.call-update) | async-done | bytes 2097168 | tf_op jit(solution)/shard_map/all_gather | solution.py:134
  164.3 5.3 %fusion.10 = bf16[16,8,512]{2,1,0:T(8,128)(2,1)S(1)} fusion(bf16[128,8192]{0,1:T(8,128)(2,1)} %all-gather.8.cloned.1.call-done, bf16[8192,512]{1,0:T(8,128)(2,1)} %param.16, f32[128]{0:T(128)S(1)} %fusion.16), kind=kOutput, calls=%fused_computation.22 | convolution fusion | flops 1073872896 | bytes 10617344 | tf_op jit(solution)/shard_map/dot_general | solution.py:133
  172.0 2.4 %collective-permute-start.1 = (bf16[1,2,1,8,512]{4,3,0,1,2:T(8,128)(2,1)S(1)}, bf16[1,2,1,8,512]{4,3,0,1,2:T(8,128)(2,1)S(1)}, u32[]{:S(2)}, u32[]{:S(2)}) collective-permute-start(bf16[1,2,1,8,512]{4,3,0,1,2:T(8,128)(2,1)S(1)} %get-tuple-element.21), channel_id=1, source_target_pairs={{0,16},{8,24},{16,32},{24,40},{32,48},{40,56},{48,64},{56,72},{64,... | collective-permute-start | bytes 49160 | tf_op jit(solution)/shard_map/ppermute | solution.py:146
  176.5 3.8 %collective-permute-start.4 = (bf16[1,2,1,8,512]{4,3,0,1,2:T(8,128)(2,1)S(1)}, bf16[1,2,1,8,512]{4,3,0,1,2:T(8,128)(2,1)S(1)}, u32[]{:S(2)}, u32[]{:S(2)}) collective-permute-start(bf16[1,2,1,8,512]{4,3,0,1,2:T(8,128)(2,1)S(1)} %get-tuple-element.18), channel_id=1, source_target_pairs={{0,40},{8,48},{16,56},{24,64},{32,72},{40,80},{48,88},{56,96},{64,... | collective-permute-start | bytes 49160 | tf_op jit(solution)/shard_map/ppermute | solution.py:146
  180.3 1.8 collective-permute-start.5
  183.7 2.0 collective-permute-start.7
  185.7 1.9 collective-permute-start.8
  187.6 4.0 %collective-permute-start.9 = (bf16[1,2,1,8,512]{4,3,0,1,2:T(8,128)(2,1)S(1)}, bf16[1,2,1,8,512]{4,3,0,1,2:T(8,128)(2,1)S(1)}, u32[]{:S(2)}, u32[]{:S(2)}) collective-permute-start(bf16[1,2,1,8,512]{4,3,0,1,2:T(8,128)(2,1)S(1)} %get-tuple-element.13), channel_id=1, source_target_pairs={{0,80},{8,88},{16,96},{24,104},{32,112},{40,120},{48,0},{56,8},{64... | collective-permute-start | bytes 49160 | tf_op jit(solution)/shard_map/ppermute | solution.py:146
  192.3 5.9 %collective-permute-start.12 = (bf16[1,2,1,8,512]{4,3,0,1,2:T(8,128)(2,1)S(1)}, bf16[1,2,1,8,512]{4,3,0,1,2:T(8,128)(2,1)S(1)}, u32[]{:S(2)}, u32[]{:S(2)}) collective-permute-start(bf16[1,2,1,8,512]{4,3,0,1,2:T(8,128)(2,1)S(1)} %get-tuple-element.10), channel_id=1, source_target_pairs={{0,104},{8,112},{16,120},{24,0},{32,8},{40,16},{48,24},{56,32},{64... | collective-permute-start | bytes 49160 | tf_op jit(solution)/shard_map/ppermute | solution.py:146
  199.6 4.7 %collective-permute-done.13 = bf16[1,2,1,8,512]{4,3,0,1,2:T(8,128)(2,1)S(1)} collective-permute-done((bf16[1,2,1,8,512]{4,3,0,1,2:T(8,128)(2,1)S(1)}, bf16[1,2,1,8,512]{4,3,0,1,2:T(8,128)(2,1)S(1)}, u32[]{:S(2)}, u32[]{:S(2)}) %collective-permute-start.13) | collective-permute-done | bytes 16416 | tf_op jit(solution)/shard_map/ppermute | solution.py:146
  204.6 2.9 %scatter_custom_fusion = f32[1024,512]{1,0:T(8,128)S(1)} fusion(f32[1024,512]{1,0:T(8,128)S(1)} %copy-done.2, s32[256]{0:T(256)S(1)} %bitcast.165, bf16[256,512]{1,0:T(8,128)(2,1)S(1)} %bitcast_select_fusion.1), kind=kCustom, calls=%fused_computation.40 | custom fusion | flops 262144 | bytes 2359296 | tf_op jit(solution)/shard_map/scatter-add | solution.py:152
  (99 shorter events, 20.4 us)
Async XLA Ops:
  6.5 80.2 %copy-start = (bf16[4096,128]{1,0:T(8,128)(2,1)S(1)}, bf16[4096,128]{1,0:T(8,128)(2,1)}, u32[]{:S(2)}) copy-start(bf16[4096,128]{1,0:T(8,128)(2,1)} %param.14) | copy-start | bytes 3145732
  6.5 34.4 %all-gather.4.cloned.1.call-start = ((), (), s32[]{:S(2)}) async-start(), calls=%async_computation.1 | async-start | bytes 2359296 | tf_op jit(solution)/shard_map/all_gather | solution.py:73
  44.8 7.5 %copy-start.4 = (bf16[4096]{0:T(1024)(128)(2,1)S(1)}, bf16[4096]{0:T(1024)(128)(2,1)}, u32[]{:S(2)}) copy-start(bf16[4096]{0:T(1024)(128)(2,1)} %param.11) | copy-start | bytes 24580
  44.8 37.8 %all-to-all-start = ((bf16[2,16,8,4096]{3,2,0,1:T(8,128)(2,1)}), bf16[2,16,8,4096]{3,2,0,1:T(8,128)(2,1)S(1)}, u32[]{:S(2)}, u32[]{:S(2)}) async-start(bf16[2,16,8,4096]{3,2,0,1:T(8,128)(2,1)} %copy.43), calls=%async_computation | async-start | bytes 4194304 | tf_op jit(solution)/shard_map/all_to_all | solution.py:77
  52.2 79.5 %all-gather.6.cloned.1.call-start = ((), (), s32[]{:S(2)}) async-start(), calls=%async_computation.2 | async-start | bytes 1114112 | tf_op jit(solution)/shard_map/all_gather | solution.py:104
  87.3 2.7 %copy-start.6 = (f32[8]{0:T(128)S(1)}, f32[8]{0:T(128)}, u32[]{:S(2)}) copy-start(f32[8]{0:T(128)} %param.17) | copy-start | bytes 100
  89.7 74.6 %all-gather.8.cloned.1.call-start = ((), (), s32[]{:S(2)}) async-start(), calls=%async_computation.3 | async-start | bytes 2359296 | tf_op jit(solution)/shard_map/all_gather | solution.py:134
  136.2 3.3 %copy-start.1 = (bf16[1024,512]{1,0:T(8,128)(2,1)S(1)}, bf16[1024,512]{1,0:T(8,128)(2,1)}, u32[]{:S(2)}) copy-start(bf16[1024,512]{1,0:T(8,128)(2,1)} %param.10) | copy-start | bytes 3145732
  169.6 35.0 %copy-start.2 = (f32[1024,512]{1,0:T(8,128)S(1)}, f32[1024,512]{1,0:T(8,128)}, u32[]{:S(2)}) copy-start(f32[1024,512]{1,0:T(8,128)} %convert_element_type.45) | copy-start | bytes 6291460
  170.4 10.0 %collective-permute-start = (bf16[1,2,1,8,512]{4,3,0,1,2:T(8,128)(2,1)S(1)}, bf16[1,2,1,8,512]{4,3,0,1,2:T(8,128)(2,1)S(1)}, u32[]{:S(2)}, u32[]{:S(2)}) collective-permute-start(bf16[1,2,1,8,512]{4,3,0,1,2:T(8,128)(2,1)S(1)} %get-tuple-element.22), channel_id=1, source_target_pairs={{0,8},{8,16},{16,24},{24,32},{32,40},{40,48},{48,56},{56,64},{64,7... | collective-permute-start | bytes 49160 | tf_op jit(solution)/shard_map/ppermute | solution.py:146
  172.0 10.1 %collective-permute-start.1 = (bf16[1,2,1,8,512]{4,3,0,1,2:T(8,128)(2,1)S(1)}, bf16[1,2,1,8,512]{4,3,0,1,2:T(8,128)(2,1)S(1)}, u32[]{:S(2)}, u32[]{:S(2)}) collective-permute-start(bf16[1,2,1,8,512]{4,3,0,1,2:T(8,128)(2,1)S(1)} %get-tuple-element.21), channel_id=1, source_target_pairs={{0,16},{8,24},{16,32},{24,40},{32,48},{40,56},{48,64},{56,72},{64,... | collective-permute-start | bytes 49160 | tf_op jit(solution)/shard_map/ppermute | solution.py:146
  174.5 9.2 %collective-permute-start.2 = (bf16[1,2,1,8,512]{4,3,0,1,2:T(8,128)(2,1)S(1)}, bf16[1,2,1,8,512]{4,3,0,1,2:T(8,128)(2,1)S(1)}, u32[]{:S(2)}, u32[]{:S(2)}) collective-permute-start(bf16[1,2,1,8,512]{4,3,0,1,2:T(8,128)(2,1)S(1)} %get-tuple-element.20), channel_id=1, source_target_pairs={{0,24},{8,32},{16,40},{24,48},{32,56},{40,64},{48,72},{56,80},{64,... | collective-permute-start | bytes 49160 | tf_op jit(solution)/shard_map/ppermute | solution.py:146
  175.3 10.4 %collective-permute-start.3 = (bf16[1,2,1,8,512]{4,3,0,1,2:T(8,128)(2,1)S(1)}, bf16[1,2,1,8,512]{4,3,0,1,2:T(8,128)(2,1)S(1)}, u32[]{:S(2)}, u32[]{:S(2)}) collective-permute-start(bf16[1,2,1,8,512]{4,3,0,1,2:T(8,128)(2,1)S(1)} %get-tuple-element.19), channel_id=1, source_target_pairs={{0,32},{8,40},{16,48},{24,56},{32,64},{40,72},{48,80},{56,88},{64,... | collective-permute-start | bytes 49160 | tf_op jit(solution)/shard_map/ppermute | solution.py:146
  176.5 11.1 %collective-permute-start.4 = (bf16[1,2,1,8,512]{4,3,0,1,2:T(8,128)(2,1)S(1)}, bf16[1,2,1,8,512]{4,3,0,1,2:T(8,128)(2,1)S(1)}, u32[]{:S(2)}, u32[]{:S(2)}) collective-permute-start(bf16[1,2,1,8,512]{4,3,0,1,2:T(8,128)(2,1)S(1)} %get-tuple-element.18), channel_id=1, source_target_pairs={{0,40},{8,48},{16,56},{24,64},{32,72},{40,80},{48,88},{56,96},{64,... | collective-permute-start | bytes 49160 | tf_op jit(solution)/shard_map/ppermute | solution.py:146
  180.3 11.3 %collective-permute-start.5 = (bf16[1,2,1,8,512]{4,3,0,1,2:T(8,128)(2,1)S(1)}, bf16[1,2,1,8,512]{4,3,0,1,2:T(8,128)(2,1)S(1)}, u32[]{:S(2)}, u32[]{:S(2)}) collective-permute-start(bf16[1,2,1,8,512]{4,3,0,1,2:T(8,128)(2,1)S(1)} %get-tuple-element.17), channel_id=1, source_target_pairs={{0,48},{8,56},{16,64},{24,72},{32,80},{40,88},{48,96},{56,104},{64... | collective-permute-start | bytes 49160 | tf_op jit(solution)/shard_map/ppermute | solution.py:146
  182.1 9.5 %collective-permute-start.6 = (bf16[1,2,1,8,512]{4,3,0,1,2:T(8,128)(2,1)S(1)}, bf16[1,2,1,8,512]{4,3,0,1,2:T(8,128)(2,1)S(1)}, u32[]{:S(2)}, u32[]{:S(2)}) collective-permute-start(bf16[1,2,1,8,512]{4,3,0,1,2:T(8,128)(2,1)S(1)} %get-tuple-element.16), channel_id=1, source_target_pairs={{0,56},{8,64},{16,72},{24,80},{32,88},{40,96},{48,104},{56,112},{6... | collective-permute-start | bytes 49160 | tf_op jit(solution)/shard_map/ppermute | solution.py:146
  183.7 8.6 %collective-permute-start.7 = (bf16[1,2,1,8,512]{4,3,0,1,2:T(8,128)(2,1)S(1)}, bf16[1,2,1,8,512]{4,3,0,1,2:T(8,128)(2,1)S(1)}, u32[]{:S(2)}, u32[]{:S(2)}) collective-permute-start(bf16[1,2,1,8,512]{4,3,0,1,2:T(8,128)(2,1)S(1)} %get-tuple-element.15), channel_id=1, source_target_pairs={{0,64},{8,72},{16,80},{24,88},{32,96},{40,104},{48,112},{56,120},{... | collective-permute-start | bytes 49160 | tf_op jit(solution)/shard_map/ppermute | solution.py:146
  185.7 12.5 %collective-permute-start.8 = (bf16[1,2,1,8,512]{4,3,0,1,2:T(8,128)(2,1)S(1)}, bf16[1,2,1,8,512]{4,3,0,1,2:T(8,128)(2,1)S(1)}, u32[]{:S(2)}, u32[]{:S(2)}) collective-permute-start(bf16[1,2,1,8,512]{4,3,0,1,2:T(8,128)(2,1)S(1)} %get-tuple-element.14), channel_id=1, source_target_pairs={{0,72},{8,80},{16,88},{24,96},{32,104},{40,112},{48,120},{56,0},{6... | collective-permute-start | bytes 49160 | tf_op jit(solution)/shard_map/ppermute | solution.py:146
  187.6 10.6 %collective-permute-start.9 = (bf16[1,2,1,8,512]{4,3,0,1,2:T(8,128)(2,1)S(1)}, bf16[1,2,1,8,512]{4,3,0,1,2:T(8,128)(2,1)S(1)}, u32[]{:S(2)}, u32[]{:S(2)}) collective-permute-start(bf16[1,2,1,8,512]{4,3,0,1,2:T(8,128)(2,1)S(1)} %get-tuple-element.13), channel_id=1, source_target_pairs={{0,80},{8,88},{16,96},{24,104},{32,112},{40,120},{48,0},{56,8},{64... | collective-permute-start | bytes 49160 | tf_op jit(solution)/shard_map/ppermute | solution.py:146
  191.6 7.5 %collective-permute-start.10 = (bf16[1,2,1,8,512]{4,3,0,1,2:T(8,128)(2,1)S(1)}, bf16[1,2,1,8,512]{4,3,0,1,2:T(8,128)(2,1)S(1)}, u32[]{:S(2)}, u32[]{:S(2)}) collective-permute-start(bf16[1,2,1,8,512]{4,3,0,1,2:T(8,128)(2,1)S(1)} %get-tuple-element.12), channel_id=1, source_target_pairs={{0,88},{8,96},{16,104},{24,112},{32,120},{40,0},{48,8},{56,16},{64... | collective-permute-start | bytes 49160 | tf_op jit(solution)/shard_map/ppermute | solution.py:146
  191.7 7.5 %collective-permute-start.11 = (bf16[1,2,1,8,512]{4,3,0,1,2:T(8,128)(2,1)S(1)}, bf16[1,2,1,8,512]{4,3,0,1,2:T(8,128)(2,1)S(1)}, u32[]{:S(2)}, u32[]{:S(2)}) collective-permute-start(bf16[1,2,1,8,512]{4,3,0,1,2:T(8,128)(2,1)S(1)} %get-tuple-element.11), channel_id=1, source_target_pairs={{0,96},{8,104},{16,112},{24,120},{32,0},{40,8},{48,16},{56,24},{64... | collective-permute-start | bytes 49160 | tf_op jit(solution)/shard_map/ppermute | solution.py:146
  192.3 7.3 %collective-permute-start.12 = (bf16[1,2,1,8,512]{4,3,0,1,2:T(8,128)(2,1)S(1)}, bf16[1,2,1,8,512]{4,3,0,1,2:T(8,128)(2,1)S(1)}, u32[]{:S(2)}, u32[]{:S(2)}) collective-permute-start(bf16[1,2,1,8,512]{4,3,0,1,2:T(8,128)(2,1)S(1)} %get-tuple-element.10), channel_id=1, source_target_pairs={{0,104},{8,112},{16,120},{24,0},{32,8},{40,16},{48,24},{56,32},{64... | collective-permute-start | bytes 49160 | tf_op jit(solution)/shard_map/ppermute | solution.py:146
  198.2 6.1 %collective-permute-start.13 = (bf16[1,2,1,8,512]{4,3,0,1,2:T(8,128)(2,1)S(1)}, bf16[1,2,1,8,512]{4,3,0,1,2:T(8,128)(2,1)S(1)}, u32[]{:S(2)}, u32[]{:S(2)}) collective-permute-start(bf16[1,2,1,8,512]{4,3,0,1,2:T(8,128)(2,1)S(1)} %get-tuple-element.9), channel_id=1, source_target_pairs={{0,112},{8,120},{16,0},{24,8},{32,16},{40,24},{48,32},{56,40},{64,... | collective-permute-start | bytes 49160 | tf_op jit(solution)/shard_map/ppermute | solution.py:146
  198.2 6.1 %collective-permute-start.14 = (bf16[1,2,1,8,512]{4,3,0,1,2:T(8,128)(2,1)S(1)}, bf16[1,2,1,8,512]{4,3,0,1,2:T(8,128)(2,1)S(1)}, u32[]{:S(2)}, u32[]{:S(2)}) collective-permute-start(bf16[1,2,1,8,512]{4,3,0,1,2:T(8,128)(2,1)S(1)} %get-tuple-element.8), channel_id=1, source_target_pairs={{0,120},{8,0},{16,8},{24,16},{32,24},{40,32},{48,40},{56,48},{64,5... | collective-permute-start | bytes 49160 | tf_op jit(solution)/shard_map/ppermute | solution.py:146
  (2 other events, 4.3 us)
Sparse Core Ops, SparseCore 0:
  13.2 27.6 all-gather.3
  89.8 41.8 all-gather.5
  139.1 25.0 all-gather.7
